TPU v7x, 32 devices: a whole 2x2x4 slice. The times are simulated.
32 devices in a mesh: hop: 8 (over z, y), tensor: 4 (over x, core).
Axes of the slice: x: 2, y: 2, z: 4, core: 2. Of those that a mesh axis runs over, the one named last changes fastest.
Arguments:
- tokens: bfloat16 [3, 2048, 1024], P(None, 'hop', 'tensor'), may hold values from -17 to 17
- targets: bfloat16 [2, 2048, 1024], P(None, 'hop', 'tensor'), may hold values from -6 to 6
- w_in: bfloat16 [8, 1024, 32768], P('hop', None, 'tensor'), may hold values from -0.1875 to 0.1875
- w_out: bfloat16 [32768, 1024], P('tensor', 'hop'), may hold values from -0.03125 to 0.03125
- noise_field: bfloat16 [8, 1024, 32768], P('hop', None, 'tensor'), may hold values from -18 to 18
- step_size: float32 [8], replicated, may hold values from 0.005 to 0.02
- clip_ratio: float32 [8], replicated, may hold values from 0.5 to 2
- noise_mult: float32 [8], replicated, may hold values from 0.002 to 0.02
- plan: int32 [8], replicated, may hold values from 0 to 7, each once
- live_rows: int32 [2, 8], P(None, 'hop'), may hold values from 128 to 256
Outputs:
- predictions: bfloat16 [2048, 1024], P('hop', 'tensor')
- row_losses: float32 [2, 2048], P(None, 'hop')
Inputs may be any that keep to these rules, and one draw needn't show every extreme that they name: `plan`: each configuration names the partition that holds it in round two; every partition is named once. The first live_rows[k, g] rows of partition g are live in round k.
All inputs are finite; a program needn't handle non-finite values.
Results may differ from a plain program's by a relative error of at most 0.0085.
Values may be sent and summed in bfloat16 or wider, within the bound.
A program may use at most 192 MiB of HBM per device.

v0:
```python
import jax
import jax.numpy as jnp
from jax import lax
from jax.sharding import PartitionSpec as P

D = 1024
FF = 32768


def gelu_parts(pre_act):
    inside = 0.7978845608 * (pre_act + 0.044715 * pre_act * pre_act * pre_act)
    tangent = jnp.tanh(inside)
    output = 0.5 * pre_act * (1.0 + tangent)
    slope_value = 0.5 * (1.0 + tangent) + 0.5 * pre_act * (
        1.0 - tangent * tangent
    ) * 0.7978845608 * (1.0 + 0.134145 * pre_act * pre_act)
    return (output, slope_value)


def local(
    tokens, targets, w_in, w_out, noise_field, step_size, clip_ratio, noise_mult, plan, live_rows
):
    group_index = lax.axis_index("hop")
    gathered = lax.all_gather(tokens, "tensor", axis=2, tiled=True)

    def forward(active):
        partial_out = jnp.dot(
            active,
            lax.all_gather(w_out, "hop", axis=1, tiled=True),
            preferred_element_type=jnp.float32,
        )
        return lax.psum_scatter(partial_out, "tensor", scatter_dimension=1, tiled=True)

    def backward(backed_full):
        return lax.dot_general(
            backed_full,
            lax.all_gather(w_out, "hop", axis=1, tiled=True),
            (((1,), (1,)), ((), ())),
            preferred_element_type=jnp.float32,
        )

    def train(
        weights, inputs, wanted, noise_block, live_count, learn_rate, clip_share, noise_scale
    ):
        pre_act = jnp.dot(inputs, weights, preferred_element_type=jnp.float32)
        output, slope_value = gelu_parts(pre_act)
        result = forward(output.astype(jnp.bfloat16))
        differ = result - wanted.astype(jnp.float32)
        live_mask = (jnp.arange(inputs.shape[0], dtype=jnp.int32) < live_count).astype(jnp.float32)
        loss_part = 0.5 * jnp.sum(differ * differ, axis=1)
        backed = differ.astype(jnp.bfloat16)
        loss_total = lax.psum(loss_part, "tensor")
        backed_full = lax.all_gather(backed, "tensor", axis=1, tiled=True)
        grad_act = backward(backed_full) * slope_value
        grad_part = jnp.sum(grad_act * grad_act, axis=1)
        grad_square = lax.psum(grad_part, "tensor")
        input_square = jnp.sum(jnp.square(inputs.astype(jnp.float32)), axis=1)
        row_norms = jnp.sqrt(input_square * grad_square)
        clip_level = clip_share * jnp.sum(row_norms * live_mask) / live_count.astype(jnp.float32)
        factor = live_mask * jnp.minimum(1.0, clip_level / (row_norms + 1e-06))
        scaled = (grad_act * factor[:, None]).astype(jnp.bfloat16)
        update = lax.dot_general(
            inputs, scaled, (((0,), (0,)), ((), ())), preferred_element_type=jnp.float32
        )
        update = update + noise_scale * clip_level * noise_block.astype(jnp.float32)
        spread = lax.psum(jnp.sum(update * update), "tensor") / (D * FF)
        renewed = (
            weights.astype(jnp.float32) - learn_rate * update * lax.rsqrt(spread + 1e-06)
        ).astype(jnp.bfloat16)
        return (renewed, loss_total * live_mask)

    trained_one, loss_one = train(
        w_in[0],
        gathered[0],
        targets[0],
        noise_field[0],
        live_rows[0, 0],
        step_size[group_index],
        clip_ratio[group_index],
        noise_mult[group_index],
    )
    indices = jnp.arange(plan.shape[0], dtype=jnp.int32)
    owners = jnp.sum(
        indices[:, None] * (plan[:, None] == indices[None, :]).astype(jnp.int32), axis=0
    )
    ordered = jnp.take(
        lax.all_to_all(trained_one[None], "hop", split_axis=1, concat_axis=0, tiled=True),
        owners,
        axis=0,
    )
    arrived = lax.all_to_all(ordered, "hop", split_axis=0, concat_axis=1, tiled=True)[0]
    holder = owners[group_index]
    trained_two, loss_two = train(
        arrived,
        gathered[1],
        targets[1],
        noise_field[0],
        live_rows[1, 0],
        step_size[holder],
        clip_ratio[holder],
        noise_mult[holder],
    )
    pre_eval = jnp.dot(gathered[2], trained_two, preferred_element_type=jnp.float32)
    output, slope_value = gelu_parts(pre_eval)
    predictions = forward(output.astype(jnp.bfloat16)).astype(jnp.bfloat16)
    row_losses = jnp.stack([loss_one, loss_two])
    return (predictions, row_losses)


def solution(mesh):
    return jax.shard_map(
        local,
        mesh=mesh,
        in_specs=(
            P(None, "hop", "tensor"),
            P(None, "hop", "tensor"),
            P("hop", None, "tensor"),
            P("tensor", "hop"),
            P("hop", None, "tensor"),
            P(),
            P(),
            P(),
            P(),
            P(None, "hop"),
        ),
        out_specs=(P("hop", "tensor"), P(None, "hop")),
        check_vma=False,
    )
```

profile of v0, /device:TPU:0, one launch (start us, length us, event | category | flops | bytes accessed | tf_op | source)
XLA Modules:
  0.0 1610.8 jit_solution(14221805219965196763)
XLA Ops:
  7.2 0.7 all-gather.3.cloned.1.call-update
  7.9 0.7 all-gather.5.cloned.1.call-update
  8.7 23.4 %all-gather.3.cloned.1.call-done = bf16[3,256,1024]{2,1,0:T(8,128)(2,1)} async-done(((bf16[3,256,256]{2,1,0:T(8,128)(2,1)}), bf16[3,256,1024]{2,1,0:T(8,128)(2,1)}) %all-gather.3.cloned.1.call-update) | async-done | bytes 1572880 | tf_op jit(solution)/shard_map/all_gather | solution.py:24
  32.1 14.0 fusion.5
  46.1 215.8 %all-gather.5.cloned.1.call-done = bf16[8192,1024]{1,0:T(8,128)(2,1)} async-done(((bf16[8192,128]{1,0:T(8,128)(2,1)}), bf16[8192,1024]{1,0:T(8,128)(2,1)}) %all-gather.5.cloned.1.call-update) | async-done | bytes 16777232 | tf_op jit(solution)/shard_map/all_gather | solution.py:29
  262.0 14.4 fusion.24
  278.4 22.5 %copy.35 = bf16[1,1024,8192]{1,2,0:T(8,128)(2,1)} copy(bf16[1,1024,8192]{2,1,0:T(8,128)(2,1)} %param.12) | data formatting | bytes 33554432 | tf_op args[2]
  300.9 22.6 %copy.36 = bf16[1,1024,8192]{1,2,0:T(8,128)(2,1)} copy(bf16[1,1024,8192]{2,1,0:T(8,128)(2,1)} %param.14) | data formatting | bytes 33554432 | tf_op args[4]
  323.5 0.6 fusion.59
  326.0 0.7 fusion.57
  326.6 0.8 multiply_reduce_fusion.4
  327.4 1.0 fusion.39
  328.4 7.6 all_gather.18
  336.0 15.7 multiply_reduce_fusion.3
  351.6 6.4 psum.42
  358.0 1.2 select_reduce_fusion.2
  361.9 23.7 %multiply_reduce_fusion.1 = (f32[]{:T(128)}, f32[8192,1024]{1,0:T(8,128)}) fusion(bf16[1,1024,8192]{1,2,0:T(8,128)(2,1)} %copy.36, f32[]{:T(128)S(6)} %mul.254, bf16[3,256,1024]{2,1,0:T(8,128)(2,1)S(1)} %copy-done.2, f32[256,8192]{1,0:T(8,128)} %get-tuple-element.21, f32[256]{0:T(256)S(1)} %minimum_select_fusion.1), kind=kOutput, calls=%fused_computation.11 | convolution fusion | flops 4341104640 | bytes 59245576 | tf_op jit(solution)/shard_map/dot_general | solution.py:62
  385.6 6.5 psum.43
  392.8 28.2 %fusion.4 = bf16[1,1024,8192]{1,2,0:T(8,128)(2,1)} fusion(bf16[1,1024,8192]{1,2,0:T(8,128)(2,1)} %copy.36, f32[8192,1024]{1,0:T(8,128)} %get-tuple-element.23, bf16[1,1024,8192]{1,2,0:T(8,128)(2,1)} %copy.35, f32[]{:T(128)S(6)} %rsqrt.6, f32[]{:T(128)S(6)} %mul.254, f32[]{:T(128)} %bitcast.1), kind=kLoop, calls=%fused_computation.12 | loop fusion | flops 67108864 | bytes 83886096 | tf_op jit(solution)/shard_map/broadcast_in_dim | solution.py:87
  420.9 67.3 %copy.37 = bf16[1,1024,8192]{2,0,1:T(2,128)(2,1)} copy(bf16[1,1024,8192]{1,2,0:T(8,128)(2,1)} %fusion.4) | data formatting | bytes 33554432 | tf_op jit(solution)/shard_map/broadcast_in_dim | solution.py:87
  488.8 100.4 %reduce = bf16[1024,8192]{1,0:T(8,128)(2,1)} reduce(bf16[1024,1,8192]{2,1,0:T(2,128)(2,1)} %bitcast.118, bf16[]{:T(256)} %broadcast.157), dimensions={1}, to_apply=%bitcast.102.reduce_sub_computation | reduce | bytes 33554432
  589.1 18.1 %reshape.59 = bf16[8,2,524288]{2,1,0:T(2,128)(2,1)} reshape(bf16[1024,8192]{1,0:T(8,128)(2,1)} %reduce) | data formatting | bytes 33554432
  607.2 5.7 all-to-all-start
  613.3 362.8 %all-to-all-done = bf16[8,2,524288]{2,1,0:T(2,128)(2,1)} async-done(((bf16[8,2,524288]{2,1,0:T(2,128)(2,1)}), bf16[8,2,524288]{2,1,0:T(2,128)(2,1)}, u32[]{:S(2)}, u32[]{:S(2)}) %all-to-all-start) | async-done | bytes 16777248 | tf_op jit(solution)/shard_map/all_to_all | solution.py:87
  976.1 22.3 %reshape.60 = bf16[1024,1,8192]{2,1,0:T(2,128)(2,1)} reshape(bf16[8,2,524288]{2,1,0:T(2,128)(2,1)} %all-to-all-done) | data formatting | bytes 33554432
  998.4 28.2 %copy.44 = bf16[1,1024,8192]{2,1,0:T(8,128)(2,1)S(1)} copy(bf16[1,1024,8192]{2,0,1:T(2,128)(2,1)} %bitcast.119) | data formatting | bytes 33554432
  1026.7 6.3 fusion.56
  1032.9 8.1 gather_fusion.1
  1041.0 8.0 gather_fusion
  1049.0 14.7 maximum_select_fusion
  1063.7 367.8 %all_to_all.21 = bf16[8,128,8192]{2,1,0:T(8,128)(2,1)S(1)} all-to-all(bf16[8,128,8192]{2,1,0:T(8,128)(2,1)} %maximum_select_fusion), channel_id=1, replica_groups=mesh['hop'=8,'tensor'=4] {'hop'}, dimensions={0} | all-to-all | bytes 33554432 | tf_op jit(solution)/shard_map/all_to_all | solution.py:91
  1431.5 5.7 copy-done
  1437.2 5.5 convolution_bitcast_fusion
  1442.8 3.2 copy-done.1
  1446.0 12.1 fusion.26
  1458.8 22.6 %copy.43 = bf16[1024,8192]{0,1:T(8,128)(2,1)} copy(bf16[1024,8192]{1,0:T(8,128)(2,1)} %bitcast.117) | data formatting | bytes 33554432 | tf_op jit(solution)/shard_map/squeeze | solution.py:91
  1481.4 1.1 multiply_reduce_fusion.7
  1482.5 7.0 all_gather.19
  1489.6 15.8 multiply_reduce_fusion.2
  1505.4 6.4 psum.44
  1511.8 1.2 select_reduce_fusion.1
  1514.3 0.6 minimum_select_fusion
  1515.6 23.7 %multiply_reduce_fusion = (f32[]{:T(128)}, f32[8192,1024]{1,0:T(8,128)}) fusion(bf16[1,1024,8192]{1,2,0:T(8,128)(2,1)} %copy.36, f32[]{:T(128)S(6)} %mul.284, bf16[3,256,1024]{2,1,0:T(8,128)(2,1)S(1)} %copy-done.3, f32[256,8192]{1,0:T(8,128)} %get-tuple-element.25, f32[256]{0:T(256)S(1)} %minimum_select_fusion), kind=kOutput, calls=%fused_computation.9 | convolution fusion | flops 4341104640 | bytes 59245576 | tf_op jit(solution)/shard_map/dot_general | solution.py:62
  1539.3 6.3 all-reduce
  1546.2 30.9 %fusion.38 = f32[256,1024]{1,0:T(8,128)} fusion(bf16[8192,1024]{1,0:T(8,128)(2,1)} %all-gather.5.cloned.1.call-done, bf16[1024,8192]{0,1:T(8,128)(2,1)} %copy.43, bf16[1,1024,8192]{1,2,0:T(8,128)(2,1)} %copy.36, f32[8192,1024]{1,0:T(8,128)} %get-tuple-element.27, f32[]{:T(128)S(6)} %rsqrt.7, f32[]{:T(128)S(6)} %mul.284, f32[]{:T(128)} %bitcast.14, ...), kind=kOutput, calls=%fused_computation.61 | convolution fusion | flops 8675917824 | bytes 85458960 | tf_op jit(solution)/shard_map/dot_general | solution.py:27
  1577.2 0.6 fusion.41
  1579.0 23.5 %reduce-scatter.8.cloned.1.call-done = f32[256,256]{1,0:T(8,128)} async-done(((f32[256,1024]{1,0:T(8,128)}), f32[256,256]{1,0:T(8,128)}) %reduce-scatter.8.cloned.1.call-update) | async-done | bytes 262160 | tf_op jit(solution)/shard_map/reduce_scatter | solution.py:32
  1602.5 1.6 convert_element_type.88
  (46 shorter events, 4.1 us)
Async XLA Ops:
  7.2 25.0 %all-gather.3.cloned.1.call-start = ((), (), s32[]{:S(2)}) async-start(), calls=%async_computation.5 | async-start | bytes 1966080 | tf_op jit(solution)/shard_map/all_gather | solution.py:24
  7.9 254.1 %all-gather.5.cloned.1.call-start = ((), (), s32[]{:S(2)}) async-start(), calls=%async_computation.6 | async-start | bytes 18874368 | tf_op jit(solution)/shard_map/all_gather | solution.py:29
  8.6 318.8 %reduce-scatter.4.cloned.1.call-start = ((), (), s32[]{:S(2)}) async-start(), calls=%async_computation.7 | async-start | bytes 1310720 | tf_op jit(solution)/shard_map/reduce_scatter | solution.py:32
  46.1 230.3 %copy-start.12 = (s32[8]{0:T(128)S(1)}, s32[8]{0:T(128)}, u32[]{:S(2)}) copy-start(s32[8]{0:T(128)} %param.18) | copy-start | bytes 100
  300.9 22.6 %copy-start.11 = (s32[2,1]{0,1:T(1,128)S(1)}, s32[2,1]{0,1:T(1,128)}, u32[]{:S(2)}) copy-start(s32[2,1]{0,1:T(1,128)} %param.19) | copy-start | bytes 28
  300.9 24.4 %copy-start.8 = (f32[8]{0:T(128)S(1)}, f32[8]{0:T(128)}, u32[]{:S(2)}) copy-start(f32[8]{0:T(128)} %param.16) | copy-start | bytes 100
  300.9 25.1 %copy-start.9 = (f32[8]{0:T(128)S(1)}, f32[8]{0:T(128)}, u32[]{:S(2)}) copy-start(f32[8]{0:T(128)} %param.15) | copy-start | bytes 100
  300.9 25.1 %copy-start.10 = (f32[8]{0:T(128)S(1)}, f32[8]{0:T(128)}, u32[]{:S(2)}) copy-start(f32[8]{0:T(128)} %param.17) | copy-start | bytes 100
  300.9 25.7 %copy-start.2 = (bf16[3,256,1024]{2,1,0:T(8,128)(2,1)S(1)}, bf16[3,256,1024]{2,1,0:T(8,128)(2,1)}, u32[]{:S(2)}) copy-start(bf16[3,256,1024]{2,1,0:T(8,128)(2,1)} %all-gather.3.cloned.1.call-done) | copy-start | bytes 4718596
  300.9 26.5 %copy-start.5 = (bf16[2,256,256]{2,1,0:T(8,128)(2,1)S(1)}, bf16[2,256,256]{2,1,0:T(8,128)(2,1)}, u32[]{:S(2)}) copy-start(bf16[2,256,256]{2,1,0:T(8,128)(2,1)} %param.11) | copy-start | bytes 786436
  607.2 368.9 %all-to-all-start = ((bf16[8,2,524288]{2,1,0:T(2,128)(2,1)}), bf16[8,2,524288]{2,1,0:T(2,128)(2,1)}, u32[]{:S(2)}, u32[]{:S(2)}) async-start(bf16[8,2,524288]{2,1,0:T(2,128)(2,1)} %reshape.59), calls=%async_computation.1 | async-start | bytes 33554432 | tf_op jit(solution)/shard_map/all_to_all | solution.py:87
  613.0 868.4 %reduce-scatter.6.cloned.1.call-start = ((), (), s32[]{:S(2)}) async-start(), calls=%async_computation.8 | async-start | bytes 1310720 | tf_op jit(solution)/shard_map/reduce_scatter | solution.py:32
  1431.5 5.7 copy-start
  1442.8 3.2 copy-start.1
  1458.1 144.3 %reduce-scatter.8.cloned.1.call-start = ((), (), s32[]{:S(2)}) async-start(), calls=%async_computation.9 | async-start | bytes 1310720 | tf_op jit(solution)/shard_map/reduce_scatter | solution.py:32
  1458.8 22.6 %copy-start.4 = (f32[256,256]{1,0:T(8,128)S(1)}, f32[256,256]{1,0:T(8,128)}, u32[]{:S(2)}) copy-start(f32[256,256]{1,0:T(8,128)} %reduce-scatter.4.cloned.1.call-done) | copy-start | bytes 786436
  1458.8 22.6 %copy-start.6 = (bf16[2,256,256]{2,1,0:T(8,128)(2,1)S(1)}, bf16[2,256,256]{2,1,0:T(8,128)(2,1)}, u32[]{:S(2)}) copy-start(bf16[2,256,256]{2,1,0:T(8,128)(2,1)} %param.11) | copy-start | bytes 786436
  1489.6 22.2 %copy-start.7 = (f32[256]{0:T(256)S(1)}, f32[256]{0:T(256)}, u32[]{:S(2)}) copy-start(f32[256]{0:T(256)} %get-tuple-element.2) | copy-start | bytes 3076
  1489.6 26.0 %copy-start.3 = (bf16[3,256,1024]{2,1,0:T(8,128)(2,1)S(1)}, bf16[3,256,1024]{2,1,0:T(8,128)(2,1)}, u32[]{:S(2)}) copy-start(bf16[3,256,1024]{2,1,0:T(8,128)(2,1)} %all-gather.3.cloned.1.call-done) | copy-start | bytes 4718596
Sparse Core Ops, SparseCore 0:
  9.5 22.5 all-gather.2
  34.2 227.7 all-gather.4
  276.5 23.0 reduce-scatter.3
  1458.2 22.8 reduce-scatter.5
  1577.3 25.1 reduce-scatter.7
where the time goes:
time: 1620 us; the launch traced here: 1610 us
  waiting for transfers between devices  627 us (39%)
  blocking collectives  408 us (25%)
  local copies, waits for them, and re-layouts  238 us (15%)
  matrix products  156 us (10%)
  other arithmetic  153 us (9%)
  between operations  22.6 us (1%)
    all_to_all x1, blocking collectives, local(): lax.all_to_all(ordered, 'hop', split_axis=0, concat_axis=1, tiled=True)[0]  368 us
    all_to_all x1, waiting for transfers between devices, local(): lax.all_to_all(trained_one[None], 'hop', split_axis=1, concat_axis=0, til...  363 us
    all_gather x1, waiting for transfers between devices, forward(): lax.all_gather(w_out, 'hop', axis=1, tiled=True)  216 us
    unnamed x32, local copies, waits for them, and re-layouts  123 us
    unnamed x1, other arithmetic  100 us
    broadcast_in_dim x1, local copies, waits for them, and re-layouts, local(): trained_one[None]  67.3 us
    dot_general x3, matrix products, forward(): jnp.dot(active, lax.all_gather(w_out, 'hop', axis=1, tiled=True), preferr...  57.4 us
    dot_general x2, matrix products, train(): lax.dot_general(inputs, scaled, (((0,), (0,)), ((), ())), preferred_eleme...  47.4 us
  transfers between devices with their start and end apart: 6, of which 4 were waited for; matrix products, arithmetic and copies ran while one was open for 5% of the time, Pallas kernels for 0%

commit v1 on v0

v1 whole, which is shorter than its diff:
```python
import jax
import jax.numpy as jnp
from jax import lax
from jax.sharding import PartitionSpec as P

BF = jnp.bfloat16
F32 = jnp.float32


def gelu_parts(pre_act):
    inside = 0.7978845608 * (pre_act + 0.044715 * pre_act * pre_act * pre_act)
    tangent = jnp.tanh(inside)
    output = 0.5 * pre_act * (1.0 + tangent)
    slope_value = 0.5 * (1.0 + tangent) + 0.5 * pre_act * (
        1.0 - tangent * tangent
    ) * 0.7978845608 * (1.0 + 0.134145 * pre_act * pre_act)
    return (output, slope_value)


def dot(a, b):
    return jnp.dot(a, b, preferred_element_type=F32)


def row_products(a, b):
    return lax.dot_general(a, b, (((1,), (1,)), ((), ())), preferred_element_type=F32)


def fine_dot(gram, b):
    high = gram.astype(BF)
    low = (gram - high.astype(F32)).astype(BF)
    both = dot(jnp.concatenate([high, low], axis=1), jnp.concatenate([b, b], axis=0))
    return both


def pick(array, index):
    return lax.dynamic_index_in_dim(array, index, 0, keepdims=False)


def local(
    tokens, targets, w_in, w_out, noise_field, step_size, clip_ratio, noise_mult, plan, live_rows
):
    hops = plan.shape[0]
    me = lax.axis_index("hop")
    rows, cols = tokens.shape[1], w_in.shape[2]
    weights, noise = w_in[0], noise_field[0]
    indices = jnp.arange(hops, dtype=jnp.int32)
    owners = jnp.sum(
        indices[:, None] * (plan[:, None] == indices[None, :]).astype(jnp.int32), axis=0
    )
    goes_to = pick(plan, me)
    holder = pick(owners, me)

    own = lax.all_gather(tokens, "tensor", axis=2, tiled=True)
    near = jnp.concatenate([tokens[1:], targets[1:]], axis=0)
    theirs = pick(lax.all_gather(near, "hop", axis=0), goes_to)
    next_rows = lax.all_gather(theirs[:2], "tensor", axis=2, tiled=True)
    next_wanted = theirs[2]
    all_w_out = lax.all_gather(w_out, "hop", axis=1, tiled=True)

    depth = own.shape[2]
    travels = dot(own[1:].reshape(2 * rows, depth), noise).astype(BF)
    block = 2 * rows // hops
    spread_out = lax.all_to_all(
        travels.reshape(hops, block, cols), "hop", split_axis=0, concat_axis=0, tiled=True
    )
    ordered = jnp.stack([pick(spread_out, plan[c]) for c in range(hops)])
    arrived = lax.all_to_all(ordered, "hop", split_axis=0, concat_axis=0, tiled=True)
    arrived = arrived.reshape(2, rows, cols)

    noise_square = jnp.sum(jnp.square(noise.astype(F32)))
    facts = jnp.stack([live_rows[1, 0].astype(F32), noise_square])
    next_facts = pick(lax.all_gather(facts, "hop", axis=0), goes_to)

    first = own[0]
    second, third = next_rows[0], next_rows[1]
    stacked = jnp.concatenate([first, second, third], axis=0)
    by_weights = dot(stacked, weights)
    by_noise = dot(stacked, noise)

    learn_rate, clip_share, noise_scale = (
        pick(step_size, me),
        pick(clip_ratio, me),
        pick(noise_mult, me),
    )
    entries = depth * cols * lax.axis_size("tensor")

    def forward(active):
        return lax.psum_scatter(dot(active, all_w_out), "tensor", scatter_dimension=1, tiled=True)

    def train(pre_act, inputs, wanted, live_count, noise_products, noise_energy):
        output, slope_value = gelu_parts(pre_act)
        differ = forward(output.astype(BF)) - wanted.astype(F32)
        live_mask = (jnp.arange(rows, dtype=jnp.int32) < live_count).astype(F32)
        loss_part = 0.5 * jnp.sum(differ * differ, axis=1)
        backed = lax.all_gather(differ.astype(BF), "tensor", axis=1, tiled=True)
        grad_act = row_products(backed, all_w_out) * slope_value
        grad_part = jnp.sum(grad_act * grad_act, axis=1)
        sums = lax.psum(jnp.stack([loss_part, grad_part]), "tensor")
        input_square = jnp.sum(jnp.square(inputs.astype(F32)), axis=1)
        row_norms = jnp.sqrt(input_square * sums[1])
        clip_level = clip_share * jnp.sum(row_norms * live_mask) / live_count.astype(F32)
        factor = live_mask * jnp.minimum(1.0, clip_level / (row_norms + 1e-06))
        scaled = (grad_act * factor[:, None]).astype(BF)
        level = noise_scale * clip_level
        inner = fine_dot(row_products(inputs, inputs), scaled)
        wide = scaled.astype(F32)
        part = jnp.sum(wide * (inner + (2.0 * level) * noise_products.astype(F32)))
        spread = lax.psum(part + level * level * noise_energy, "tensor") / entries
        step = learn_rate * lax.rsqrt(spread + 1e-06)
        return scaled, level, step, sums[0] * live_mask

    scaled_one, level_one, step_one, loss_one = train(
        by_weights[:rows], first, targets[0], live_rows[0, 0], by_noise[:rows], noise_square
    )
    moved = fine_dot(row_products(stacked[rows:], first), scaled_one)
    pre_both = by_weights[rows:] - step_one * (moved + level_one * by_noise[rows:])
    scaled_two, level_two, step_two, loss_two = train(
        pre_both[:rows],
        second,
        next_wanted,
        next_facts[0].astype(jnp.int32),
        arrived[0],
        next_facts[1],
    )
    moved = fine_dot(row_products(third, second), scaled_two)
    pre_eval = pre_both[rows:] - step_two * (moved + level_two * arrived[1].astype(F32))
    output, slope_value = gelu_parts(pre_eval)
    outcome = forward(output.astype(BF)).astype(BF)
    predictions = pick(lax.all_gather(outcome, "hop", axis=0), holder)
    loss_two = pick(lax.all_gather(loss_two, "hop", axis=0), holder)
    return (predictions, jnp.stack([loss_one, loss_two]))


def solution(mesh):
    return jax.shard_map(
        local,
        mesh=mesh,
        in_specs=(
            P(None, "hop", "tensor"),
            P(None, "hop", "tensor"),
            P("hop", None, "tensor"),
            P("tensor", "hop"),
            P("hop", None, "tensor"),
            P(),
            P(),
            P(),
            P(),
            P(None, "hop"),
        ),
        out_specs=(P("hop", "tensor"), P(None, "hop")),
        check_vma=False,
    )
```

time: 1620 us -> 880 us (0.54)
  blocking collectives: 408 us -> 102 us
  local copies, waits for them, and re-layouts: 238 us -> 32 us
  waiting for transfers between devices: 627 us -> 472 us
  other arithmetic: 153 us -> 39.6 us
  between operations: 22.6 us -> 45.1 us
  matrix products: 156 us -> 173 us
    all_to_all x1 -> x0, blocking collectives: 368 us -> none  [local(): lax.all_to_all(ordered, 'hop', split_axis=0, concat_axis=1, tiled=True)[0]]
    all_to_all x1 -> x2, waiting for transfers between devices: 363 us -> 250 us  [the longest x1 250 us: local(): lax.all_to_all(travels.reshape(hops, block, cols), 'hop', split_axis=0, c...]
    unnamed x32 -> x29, local copies, waits for them, and re-layouts: 123 us -> 16.7 us
    unnamed x1 -> x2, other arithmetic: 100 us -> 0.8 us
    all_gather x2 -> x5, waiting for transfers between devices: 239 us -> 146 us  [the longest x1 59 us: local(): theirs = pick(lax.all_gather(near, 'hop', axis=0), goes_to)]
    broadcast_in_dim x1 -> x0, local copies, waits for them, and re-layouts: 67.3 us -> none  [local(): trained_one[None]]
    reduce_scatter x3, waiting for transfers between devices: 23.5 us -> 75.2 us  [forward(): lax.psum_scatter(dot(active, all_w_out), 'tensor', scatter_dimension=1, t...]
    unnamed x0 -> x1, blocking collectives: none -> 41.4 us
  transfers between devices with their start and end apart: 6 -> 10, of which waited for: 4 -> 7; matrix products, arithmetic and copies ran while one was open for 5% -> 22% of each run, Pallas kernels for 0% -> 0%
where the time goes in v1:
time: 880 us; the launch traced here: 876 us
  waiting for transfers between devices  472 us (54%)
  matrix products  173 us (20%)
  blocking collectives  102 us (12%)
  between operations  45.1 us (5%)
  other arithmetic  39.6 us (4%)
  local copies, waits for them, and re-layouts  32 us (4%)
  starting transfers between devices  11.6 us (1%)
    all_to_all x1, waiting for transfers between devices, local(): lax.all_to_all(travels.reshape(hops, block, cols), 'hop', split_axis=0, c...  250 us
    dot_general x9, matrix products, dot(): return jnp.dot(a, b, preferred_element_type=F32)  140 us
    reduce_scatter x3, waiting for transfers between devices, forward(): lax.psum_scatter(dot(active, all_w_out), 'tensor', scatter_dimension=1, t...  75.2 us
    all_gather x1, waiting for transfers between devices, local(): theirs = pick(lax.all_gather(near, 'hop', axis=0), goes_to)  59 us
    all_gather x1, waiting for transfers between devices, local(): all_w_out = lax.all_gather(w_out, 'hop', axis=1, tiled=True)  51.4 us
    unnamed x1, blocking collectives  41.4 us
    dot_general x6, matrix products, row_products(): lax.dot_general(a, b, (((1,), (1,)), ((), ())), preferred_element_type=F32)  33.1 us
    all_gather x1, blocking collectives, local(): loss_two = pick(lax.all_gather(loss_two, 'hop', axis=0), holder)  20.5 us
  transfers between devices with their start and end apart: 10, of which 7 were waited for; matrix products, arithmetic and copies ran while one was open for 22% of the time, Pallas kernels for 0%

profile of v1, /device:TPU:0, one launch (start us, length us, event | category | flops | bytes accessed | tf_op | source)
XLA Modules:
  0.0 875.7 jit_solution(1757339928340333789)
XLA Ops:
  10.7 1.7 fusion.93
  14.3 59.0 %all-gather.15.cloned.1.call-done = bf16[24,256,256]{2,1,0:T(8,128)(2,1)} async-done(((bf16[3,256,256]{2,1,0:T(8,128)(2,1)}), bf16[24,256,256]{2,1,0:T(8,128)(2,1)}) %all-gather.15.cloned.1.call-update) | async-done | bytes 3145744 | tf_op jit(solution)/shard_map/all_gather | solution.py:55
  73.4 1.7 constant_dynamic-slice_fusion
  75.6 17.8 %all-gather.11.cloned.1.call-done = bf16[3,256,1024]{2,1,0:T(8,128)(2,1)} async-done(((bf16[3,256,256]{2,1,0:T(8,128)(2,1)}), bf16[3,256,1024]{2,1,0:T(8,128)(2,1)}) %all-gather.11.cloned.1.call-update) | async-done | bytes 1572880 | tf_op jit(solution)/shard_map/all_gather | solution.py:53
  93.4 1.3 slice.156
  94.7 16.8 %fusion.9 = bf16[512,8192]{1,0:T(8,128)(2,1)} fusion(bf16[512,1024]{1,0:T(8,128)(2,1)S(1)} %bitcast.95, bf16[1,1024,8192]{2,1,0:T(8,128)(2,1)} %param.14), kind=kOutput, calls=%fused_computation.16 | convolution fusion | flops 8594128896 | bytes 26214400 | tf_op jit(solution)/shard_map/dot_general | solution.py:21
  111.5 5.7 all-to-all-start
  135.9 11.0 %multiply_reduce_fusion = f32[]{:T(128)} fusion(bf16[1,1024,8192]{2,1,0:T(8,128)(2,1)} %param.14), kind=kLoop, calls=%fused_computation | loop fusion | flops 25165824 | bytes 16777220 | tf_op jit(solution)/shard_map/reduce_sum | solution.py:70
  147.5 1.3 slice_bitcast_fusion.1
  148.7 21.2 %fusion.5 = f32[768,8192]{1,0:T(8,128)} fusion(bf16[1,1024,8192]{2,1,0:T(8,128)(2,1)} %param.14, bf16[256,1024]{1,0:T(8,128)(2,1)S(1)} %get-tuple-element.15, bf16[256,1024]{1,0:T(8,128)(2,1)S(1)} %get-tuple-element.14, bf16[256,1024]{1,0:T(8,128)(2,1)S(1)} %slice_bitcast_fusion.2), kind=kOutput, calls=%fused_computation.7 | convolution fusion | flops 12889620480 | bytes 43515904 | tf_op jit(solution)/shard_map/dot_general | solution.py:21
  169.9 21.3 %fusion.7 = f32[768,8192]{1,0:T(8,128)} fusion(bf16[1,1024,8192]{2,1,0:T(8,128)(2,1)} %param.12, bf16[256,1024]{1,0:T(8,128)(2,1)S(1)} %get-tuple-element.15, bf16[256,1024]{1,0:T(8,128)(2,1)S(1)} %get-tuple-element.14, bf16[256,1024]{1,0:T(8,128)(2,1)S(1)} %slice_bitcast_fusion.2), kind=kOutput, calls=%fused_computation.9 | convolution fusion | flops 12889620480 | bytes 43515904 | tf_op jit(solution)/shard_map/dot_general | solution.py:21
  191.2 249.8 %all-to-all-done = bf16[8,64,8192]{2,1,0:T(8,128)(2,1)} async-done(((bf16[8,64,8192]{2,1,0:T(8,128)(2,1)}), bf16[8,64,8192]{2,1,0:T(8,128)(2,1)}, u32[]{:S(2)}, u32[]{:S(2)}) %all-to-all-start) | async-done | bytes 8388640 | tf_op jit(solution)/shard_map/all_to_all | solution.py:63
  441.0 2.4 dynamic-slice_dynamic-update-slice_fusion.7
  443.4 2.3 dynamic-slice_dynamic-update-slice_fusion.6
  445.6 2.3 dynamic-slice_dynamic-update-slice_fusion.5
  447.9 2.3 dynamic-slice_dynamic-update-slice_fusion.4
  450.2 2.4 dynamic-slice_dynamic-update-slice_fusion.3
  452.6 51.4 %all-gather.13.cloned.1.call-done = bf16[8192,1024]{1,0:T(8,128)(2,1)} async-done(((bf16[8192,128]{1,0:T(8,128)(2,1)}), bf16[8192,1024]{1,0:T(8,128)(2,1)}) %all-gather.13.cloned.1.call-update) | async-done | bytes 16777232 | tf_op jit(solution)/shard_map/all_gather | solution.py:58
  504.0 14.4 %fusion.31 = f32[256,1024]{1,0:T(8,128)} fusion(bf16[8192,1024]{1,0:T(8,128)(2,1)} %all-gather.13.cloned.1.call-done, f32[768,8192]{1,0:T(8,128)} %fusion.7), kind=kOutput, calls=%fused_computation.52 | convolution fusion | flops 4313841664 | bytes 26214400 | tf_op jit(solution)/shard_map/dot_general | solution.py:21
  518.4 2.3 dynamic-slice_dynamic-update-slice_fusion.2
  520.7 2.3 dynamic-slice_dynamic-update-slice_fusion.1
  522.9 2.3 dynamic-slice_dynamic-update-slice_fusion
  525.2 5.1 all-to-all-start.1
  530.3 12.3 %reduce-scatter.4.cloned.1.call-done = f32[256,256]{1,0:T(8,128)} async-done(((f32[256,1024]{1,0:T(8,128)}), f32[256,256]{1,0:T(8,128)}) %reduce-scatter.4.cloned.1.call-update) | async-done | bytes 262160 | tf_op jit(solution)/shard_map/reduce_scatter | solution.py:88
  543.7 6.8 all_gather.42
  550.5 15.7 %multiply_reduce_fusion.2 = (f32[256]{0:T(256)S(1)}, f32[256,8192]{1,0:T(8,128)}) fusion(f32[768,8192]{1,0:T(8,128)} %fusion.7, bf16[256,1024]{1,0:T(8,128)(2,1)S(1)} %all_gather.42, bf16[8192,1024]{1,0:T(8,128)(2,1)} %all-gather.13.cloned.1.call-done), kind=kOutput, calls=%fused_computation.50 | convolution fusion | flops 4336910336 | bytes 34079744 | tf_op jit(solution)/shard_map/dot_general | solution.py:25
  566.2 7.1 psum.28
  574.0 1.2 select_reduce_fusion.2
  577.2 6.2 multiply_convert_fusion.2
  584.7 9.6 %fusion.43 = f32[]{:T(128)} fusion(f32[768,8192]{1,0:T(8,128)} %fusion.5, f32[]{:T(128)S(6)} %mul.307, bf16[256,8192]{1,0:T(8,128)(2,1)} %multiply_convert_fusion.2, bf16[256,256]{0,1:T(8,128)(2,1)S(1)} %get-tuple-element.8, bf16[256,256]{0,1:T(8,128)(2,1)S(1)} %get-tuple-element.9), kind=kOutput, calls=%fused_computation.64 | convolution fusion | flops 2175270912 | bytes 17039368 | tf_op jit(solution)/shard_map/dot_general | solution.py:21
  595.4 6.6 psum.29
  603.3 20.0 %fusion.2 = f32[512,8192]{1,0:T(8,128)} fusion(f32[768,8192]{1,0:T(8,128)} %fusion.5, f32[768,8192]{1,0:T(8,128)} %fusion.7, f32[]{:T(128)S(6)} %mul.306, f32[]{:T(128)S(6)} %mul.313, bf16[256,8192]{1,0:T(8,128)(2,1)} %multiply_convert_fusion.2, bf16[512,256]{0,1:T(8,128)(2,1)S(1)} %get-tuple-element.6, bf16[512,256]{0,1:T(8,128)(2,1)S(1)} %get-tuple-element.7), kind=kOutput, calls=%fused_computation.4 | convolution fusion | flops 4329570304 | bytes 55050248 | tf_op jit(solution)/shard_map/dot_general | solution.py:21
  623.3 14.5 %fusion.32 = f32[256,1024]{1,0:T(8,128)} fusion(bf16[8192,1024]{1,0:T(8,128)(2,1)} %all-gather.13.cloned.1.call-done, f32[512,8192]{1,0:T(8,128)} %fusion.2), kind=kOutput, calls=%fused_computation.53 | convolution fusion | flops 4313841664 | bytes 26214400 | tf_op jit(solution)/shard_map/dot_general | solution.py:21
  640.6 41.4 %all-reduce.1 = f32[8,2]{1,0:T(8,128)S(1)} all-reduce(f32[8,2]{1,0:T(8,128)S(1)} %reshape.106), channel_id=4, replica_groups=mesh['hop'=8,'tensor'=4] {'hop'}, use_global_device_ids=true, to_apply=%add | all-reduce | flops 16 | bytes 128
  683.7 1.1 multiply_reduce_fusion.5
  684.8 6.5 all_gather.43
  691.3 15.9 %multiply_reduce_fusion.1 = (f32[256]{0:T(256)S(1)}, f32[256,8192]{1,0:T(8,128)}) fusion(f32[512,8192]{1,0:T(8,128)} %fusion.2, bf16[256,1024]{1,0:T(8,128)(2,1)S(1)} %all_gather.43, bf16[8192,1024]{1,0:T(8,128)(2,1)} %all-gather.13.cloned.1.call-done), kind=kOutput, calls=%fused_computation.47 | convolution fusion | flops 4336910336 | bytes 34079744 | tf_op jit(solution)/shard_map/dot_general | solution.py:25
  707.2 7.2 psum.30
  717.8 6.2 multiply_convert_fusion
  724.0 6.5 convert_multiply_fusion.1
  730.5 4.8 fusion.44
  736.3 6.2 psum.31
  743.7 17.1 %fusion.39 = f32[256,1024]{1,0:T(8,128)} fusion(bf16[8192,1024]{1,0:T(8,128)(2,1)} %all-gather.13.cloned.1.call-done, f32[256,8192]{1,0:T(8,128)} %bitcast.93, f32[512,8192]{1,0:T(8,128)} %fusion.2, bf16[256,8192]{1,0:T(8,128)(2,1)} %multiply_convert_fusion, f32[]{:T(128)S(6)} %mul.350, bf16[256,256]{0,1:T(8,128)(2,1)S(1)} %get-tuple-element.2, ...), kind=kOutput, calls=%fused_computation.60 | convolution fusion | flops 6484918272 | bytes 39059460 | tf_op jit(solution)/shard_map/dot_general | solution.py:21
  760.9 62.9 %reduce-scatter.8.cloned.1.call-done = f32[256,256]{1,0:T(8,128)} async-done(((f32[256,1024]{1,0:T(8,128)}), f32[256,256]{1,0:T(8,128)}) %reduce-scatter.8.cloned.1.call-update) | async-done | bytes 262160 | tf_op jit(solution)/shard_map/reduce_scatter | solution.py:88
  823.8 1.6 convert_element_type.153
  828.1 20.5 %all-gather.4 = f32[8,1,256]{2,1,0:T(1,128)S(1)} all-gather(f32[1,1,256]{2,1,0:T(1,128)S(1)} %get-tuple-element.20), channel_id=1, replica_groups=mesh['hop'=8,'tensor'=4] {'hop'}, dimensions={0}, use_global_device_ids=true | all-gather | bytes 9216 | tf_op jit(solution)/shard_map/all_gather | solution.py:130
  849.2 17.8 %all-gather.19.cloned.1.call-done = bf16[2048,256]{1,0:T(8,128)(2,1)} async-done(((bf16[256,256]{1,0:T(8,128)(2,1)}), bf16[2048,256]{1,0:T(8,128)(2,1)}) %all-gather.19.cloned.1.call-update) | async-done | bytes 1048592 | tf_op jit(solution)/shard_map/all_gather | solution.py:129
  867.0 1.6 dynamic-slice_bitcast_fusion.1
  (73 shorter events, 15.6 us)
Async XLA Ops:
  7.2 66.2 %all-gather.15.cloned.1.call-start = ((), (), s32[]{:S(2)}) async-start(), calls=%async_computation.10 | async-start | bytes 3538944 | tf_op jit(solution)/shard_map/all_gather | solution.py:55
  9.9 83.5 %all-gather.11.cloned.1.call-start = ((), (), s32[]{:S(2)}) async-start(), calls=%async_computation.5 | async-start | bytes 1966080 | tf_op jit(solution)/shard_map/all_gather | solution.py:53
  10.7 136.8 %all-gather.17.cloned.1.call-start = ((), (), s32[]{:S(2)}) async-start(), calls=%async_computation.11 | async-start | bytes 1310720 | tf_op jit(solution)/shard_map/all_gather | solution.py:56
  75.1 428.9 %all-gather.13.cloned.1.call-start = ((), (), s32[]{:S(2)}) async-start(), calls=%async_computation.6 | async-start | bytes 18874368 | tf_op jit(solution)/shard_map/all_gather | solution.py:58
  111.5 16.3 %copy-start.6 = (f32[8]{0:T(128)S(1)}, f32[8]{0:T(128)}, u32[]{:S(2)}) copy-start(f32[8]{0:T(128)} %param.16) | copy-start | bytes 100
  111.5 16.9 %copy-start.5 = (s32[2,1]{0,1:T(1,128)S(1)}, s32[2,1]{0,1:T(1,128)}, u32[]{:S(2)}) copy-start(s32[2,1]{0,1:T(1,128)} %param.19) | copy-start | bytes 28
  111.5 18.2 %copy-start.7 = (f32[8]{0:T(128)S(1)}, f32[8]{0:T(128)}, u32[]{:S(2)}) copy-start(f32[8]{0:T(128)} %param.17) | copy-start | bytes 100
  111.5 18.8 %copy-start.8 = (f32[8]{0:T(128)S(1)}, f32[8]{0:T(128)}, u32[]{:S(2)}) copy-start(f32[8]{0:T(128)} %param.15) | copy-start | bytes 100
  111.5 329.5 %all-to-all-start = ((bf16[8,64,8192]{2,1,0:T(8,128)(2,1)}), bf16[8,64,8192]{2,1,0:T(8,128)(2,1)}, u32[]{:S(2)}, u32[]{:S(2)}) async-start(bf16[8,64,8192]{2,1,0:T(8,128)(2,1)} %bitcast.92), calls=%async_computation.2 | async-start | bytes 16777216 | tf_op jit(solution)/shard_map/all_to_all | solution.py:63
  117.2 425.5 %reduce-scatter.4.cloned.1.call-start = ((), (), s32[]{:S(2)}) async-start(), calls=%async_computation.7 | async-start | bytes 1310720 | tf_op jit(solution)/shard_map/reduce_scatter | solution.py:88
  135.9 11.0 %copy-start.1 = (bf16[3,256,1024]{2,1,0:T(8,128)(2,1)S(1)}, bf16[3,256,1024]{2,1,0:T(8,128)(2,1)}, u32[]{:S(2)}) copy-start(bf16[3,256,1024]{2,1,0:T(8,128)(2,1)} %all-gather.11.cloned.1.call-done) | copy-start | bytes 4718596
  525.2 17.4 %copy-start.3 = (bf16[2,256,256]{2,1,0:T(8,128)(2,1)S(1)}, bf16[2,256,256]{2,1,0:T(8,128)(2,1)}, u32[]{:S(2)}) copy-start(bf16[2,256,256]{2,1,0:T(8,128)(2,1)} %param.11) | copy-start | bytes 786436
  525.2 198.8 %all-to-all-start.1 = ((bf16[8,64,8192]{2,1,0:T(8,128)(2,1)}), bf16[8,64,8192]{2,1,0:T(8,128)(2,1)}, u32[]{:S(2)}, u32[]{:S(2)}) async-start(bf16[8,64,8192]{2,1,0:T(8,128)(2,1)} %dynamic-slice_dynamic-update-slice_fusion), calls=%async_computation.3 | async-start | bytes 16777216 | tf_op jit(solution)/shard_map/all_to_all | solution.py:67
  530.3 153.4 %reduce-scatter.6.cloned.1.call-start = ((), (), s32[]{:S(2)}) async-start(), calls=%async_computation.8 | async-start | bytes 1310720 | tf_op jit(solution)/shard_map/reduce_scatter | solution.py:88
  623.2 15.2 %copy-start.9 = (u32[32]{0:T(128)S(1)}, u32[32]{0:T(128)}, u32[]{:S(2)}) copy-start(u32[32]{0:T(128)} %constant.92) | copy-start | bytes 388
  623.3 59.9 %copy-start.2 = (bf16[1,2,256,1024]{3,2,1,0:T(8,128)(2,1)S(1)}, bf16[1,2,256,1024]{3,2,1,0:T(8,128)(2,1)}, u32[]{:S(2)}) copy-start(bf16[1,2,256,1024]{3,2,1,0:T(8,128)(2,1)} %all-gather.17.cloned.1.call-done) | copy-start | bytes 3145732
  637.8 186.0 %reduce-scatter.8.cloned.1.call-start = ((), (), s32[]{:S(2)}) async-start(), calls=%async_computation.9 | async-start | bytes 1310720 | tf_op jit(solution)/shard_map/reduce_scatter | solution.py:88
  724.0 6.5 copy-start
  743.7 81.7 %copy-start.4 = (s32[8]{0:T(128)S(1)}, s32[8]{0:T(128)}, u32[]{:S(2)}) copy-start(s32[8]{0:T(128)} %param.18) | copy-start | bytes 100
  760.8 106.2 %all-gather.19.cloned.1.call-start = ((), (), s32[]{:S(2)}) async-start(), calls=%async_computation.12 | async-start | bytes 1179648 | tf_op jit(solution)/shard_map/all_gather | solution.py:129
Sparse Core Ops, SparseCore 0:
  10.2 63.1 all-gather.14
  74.9 18.4 all-gather.10
  95.0 16.8 all-gather.16
  113.7 390.1 all-gather.12
  518.5 24.0 reduce-scatter.3
  637.9 25.3 reduce-scatter.5
  760.9 62.7 reduce-scatter.7
  826.7 40.2 all-gather.18

commit v2 on v1

--- a/solution.py
+++ b/solution.py
@@ -1,6 +1,8 @@
 import jax
 import jax.numpy as jnp
 from jax import lax
+from jax.experimental import pallas as pl
+from jax.experimental.pallas import tpu as pltpu
 from jax.sharding import PartitionSpec as P
 
 BF = jnp.bfloat16
@@ -32,6 +34,43 @@
     return both
 
 
+SLAB = 16
+
+
+def three_parts(values):
+    high = values.astype(BF)
+    rest = values - high.astype(F32)
+    middle = rest.astype(BF)
+    return [high, middle, (rest - middle.astype(F32)).astype(BF)]
+
+
+def after(array, other):
+    return lax.optimization_barrier((array, other))[0]
+
+
+def copy_block(order_ref, in_ref, out_ref):
+    out_ref[...] = in_ref[...]
+
+
+def reorder(blocks, order):
+    block = (1,) + blocks.shape[1:]
+    return pl.pallas_call(
+        copy_block,
+        out_shape=jax.ShapeDtypeStruct(blocks.shape, blocks.dtype),
+        grid_spec=pltpu.PrefetchScalarGridSpec(
+            num_scalar_prefetch=1,
+            grid=(blocks.shape[0],),
+            in_specs=[pl.BlockSpec(block, lambda i, order_ref: (order_ref[i], 0, 0))],
+            out_specs=pl.BlockSpec(block, lambda i, order_ref: (i, 0, 0)),
+        ),
+    )(order, blocks)
+
+
+def route(blocks, plan):
+    spread = lax.all_to_all(blocks, "hop", split_axis=0, concat_axis=0, tiled=True)
+    return lax.all_to_all(reorder(spread, plan), "hop", split_axis=0, concat_axis=0, tiled=True)
+
+
 def pick(array, index):
     return lax.dynamic_index_in_dim(array, index, 0, keepdims=False)
 
@@ -47,35 +86,38 @@
     owners = jnp.sum(
         indices[:, None] * (plan[:, None] == indices[None, :]).astype(jnp.int32), axis=0
     )
-    goes_to = pick(plan, me)
     holder = pick(owners, me)
 
-    own = lax.all_gather(tokens, "tensor", axis=2, tiled=True)
-    near = jnp.concatenate([tokens[1:], targets[1:]], axis=0)
-    theirs = pick(lax.all_gather(near, "hop", axis=0), goes_to)
-    next_rows = lax.all_gather(theirs[:2], "tensor", axis=2, tiled=True)
-    next_wanted = theirs[2]
     all_w_out = lax.all_gather(w_out, "hop", axis=1, tiled=True)
 
-    depth = own.shape[2]
-    travels = dot(own[1:].reshape(2 * rows, depth), noise).astype(BF)
-    block = 2 * rows // hops
-    spread_out = lax.all_to_all(
-        travels.reshape(hops, block, cols), "hop", split_axis=0, concat_axis=0, tiled=True
-    )
-    ordered = jnp.stack([pick(spread_out, plan[c]) for c in range(hops)])
-    arrived = lax.all_to_all(ordered, "hop", split_axis=0, concat_axis=0, tiled=True)
-    arrived = arrived.reshape(2, rows, cols)
+    def widen(block):
+        return lax.all_gather(block, "tensor", axis=1, tiled=True)
+
+    own_second = widen(tokens[1])
+    own_third = widen(after(tokens[2], own_second))
+    first = widen(after(tokens[0], own_third))
+    depth = first.shape[1]
 
     noise_square = jnp.sum(jnp.square(noise.astype(F32)))
-    facts = jnp.stack([live_rows[1, 0].astype(F32), noise_square])
-    next_facts = pick(lax.all_gather(facts, "hop", axis=0), goes_to)
+    facts = jnp.stack(three_parts(jnp.stack([live_rows[1, 0].astype(F32), noise_square])))
+    slab = jnp.zeros((hops, SLAB, tokens.shape[2]), BF).at[:, :3, :2].set(facts[None])
+    near = jnp.concatenate([tokens[1:], targets[1:]], axis=0).reshape(hops, -1, tokens.shape[2])
+    depth_near = near.shape[1]
+    landed = route(jnp.concatenate([near, slab], axis=1), plan)
+    next_facts = jnp.sum(landed[0, depth_near : depth_near + 3, :2].astype(F32), axis=0)
+    theirs = landed[:, :depth_near].reshape(3, rows, tokens.shape[2])
+    next_wanted = theirs[2]
 
-    first = own[0]
-    second, third = next_rows[0], next_rows[1]
-    stacked = jnp.concatenate([first, second, third], axis=0)
-    by_weights = dot(stacked, weights)
-    by_noise = dot(stacked, noise)
+    def products(own):
+        return dot(own, noise).astype(BF).reshape(hops, rows // hops, cols)
+
+    arrived = [route(products(own), plan).reshape(rows, cols) for own in (own_second, own_third)]
+
+    second = widen(theirs[0])
+    third = widen(after(theirs[1], second))
+    by_weights_first, by_noise_first = dot(first, weights), dot(first, noise).astype(BF)
+    later = jnp.concatenate([second, third], axis=0)
+    by_weights, by_noise = dot(later, weights), dot(later, noise)
 
     learn_rate, clip_share, noise_scale = (
         pick(step_size, me),
@@ -110,10 +152,10 @@
         return scaled, level, step, sums[0] * live_mask
 
     scaled_one, level_one, step_one, loss_one = train(
-        by_weights[:rows], first, targets[0], live_rows[0, 0], by_noise[:rows], noise_square
+        by_weights_first, first, targets[0], live_rows[0, 0], by_noise_first, noise_square
     )
-    moved = fine_dot(row_products(stacked[rows:], first), scaled_one)
-    pre_both = by_weights[rows:] - step_one * (moved + level_one * by_noise[rows:])
+    moved = fine_dot(row_products(later, first), scaled_one)
+    pre_both = by_weights - step_one * (moved + level_one * by_noise)
     scaled_two, level_two, step_two, loss_two = train(
         pre_both[:rows],
         second,
@@ -126,9 +168,14 @@
     pre_eval = pre_both[rows:] - step_two * (moved + level_two * arrived[1].astype(F32))
     output, slope_value = gelu_parts(pre_eval)
     outcome = forward(output.astype(BF)).astype(BF)
-    predictions = pick(lax.all_gather(outcome, "hop", axis=0), holder)
-    loss_two = pick(lax.all_gather(loss_two, "hop", axis=0), holder)
-    return (predictions, jnp.stack([loss_one, loss_two]))
+    width = outcome.shape[1]
+    losses = jnp.concatenate([p.reshape(-1, width) for p in three_parts(loss_two)], axis=0)
+    count = losses.shape[0]
+    losses = jnp.pad(losses, ((0, -count % SLAB), (0, 0)))
+    back = pick(lax.all_gather(jnp.concatenate([outcome, losses], axis=0), "hop", axis=0), holder)
+    predictions = back[:rows]
+    loss_back = back[rows : rows + count].astype(F32).reshape(3, rows)
+    return (predictions, jnp.stack([loss_one, jnp.sum(loss_back, axis=0)]))
 
 
 def solution(mesh):

time: 880 us -> 795 us (0.903)
  waiting for transfers between devices: 472 us -> 389 us
  matrix products: 173 us -> 199 us
  blocking collectives: 102 us -> 77.3 us
  local copies, waits for them, and re-layouts: 32 us -> 10 us
  Pallas kernels: 0 us -> 20 us
  starting transfers between devices: 11.6 us -> 30.4 us
  between operations: 45.1 us -> 27.4 us
    all_gather x1, waiting for transfers between devices: 51.4 us -> 216 us  [local(): all_w_out = lax.all_gather(w_out, 'hop', axis=1, tiled=True)]
    all_to_all x2 -> x6, waiting for transfers between devices: 250 us -> 92.6 us  [the longest x3 62.4 us: route(): lax.all_to_all(reorder(spread, plan), 'hop', split_axis=0, concat_axis=0,...]
    all_gather x4 -> x1, waiting for transfers between devices: 94.7 us -> 38.6 us  [local(): lax.all_gather(jnp.concatenate([outcome, losses], axis=0), 'hop', axis=0)]
    unnamed x1 -> x0, blocking collectives: 41.4 us -> none
    reduce_scatter x3, waiting for transfers between devices: 75.2 us -> 40.7 us  [forward(): lax.psum_scatter(dot(active, all_w_out), 'tensor', scatter_dimension=1, t...]
    dot_general x9 -> x12, matrix products: 140 us -> 165 us  [dot(): return jnp.dot(a, b, preferred_element_type=F32)]
    pallas_call x0 -> x3, Pallas kernels: none -> 20 us  [reorder(): pl.pallas_call(copy_block, out_shape=jax.ShapeDtypeStruct(blocks.shape, b...]
    all_to_all x2 -> x6, starting transfers between devices: 10.7 us -> 29.9 us  [the longest x3 17.4 us: route(): lax.all_to_all(blocks, 'hop', split_axis=0, concat_axis=0, tiled=True)]
  transfers between devices with their start and end apart: 10 -> 11, of which waited for: 7 -> 9; matrix products, arithmetic and copies ran while one was open for 22% -> 27% of each run, Pallas kernels for 0% -> 3%
where the time goes in v2:
time: 795 us; the launch traced here: 787 us
  waiting for transfers between devices  389 us (49%)
  matrix products  199 us (25%)
  blocking collectives  77.3 us (10%)
  other arithmetic  34.9 us (4%)
  starting transfers between devices  30.4 us (4%)
  between operations  27.4 us (3%)
  Pallas kernels  20 us (3%)
  local copies, waits for them, and re-layouts  10 us (1%)
    all_gather x1, waiting for transfers between devices, local(): all_w_out = lax.all_gather(w_out, 'hop', axis=1, tiled=True)  216 us
    dot_general x12, matrix products, dot(): return jnp.dot(a, b, preferred_element_type=F32)  165 us
    all_to_all x3, waiting for transfers between devices, route(): lax.all_to_all(reorder(spread, plan), 'hop', split_axis=0, concat_axis=0,...  62.4 us
    reduce_scatter x3, waiting for transfers between devices, forward(): lax.psum_scatter(dot(active, all_w_out), 'tensor', scatter_dimension=1, t...  40.7 us
    all_gather x1, waiting for transfers between devices, local(): lax.all_gather(jnp.concatenate([outcome, losses], axis=0), 'hop', axis=0)  38.6 us
    all_gather x5, blocking collectives, widen(): return lax.all_gather(block, 'tensor', axis=1, tiled=True)  36.3 us
    dot_general x6, matrix products, row_products(): lax.dot_general(a, b, (((1,), (1,)), ((), ())), preferred_element_type=F32)  33.5 us
    all_to_all x3, waiting for transfers between devices, route(): lax.all_to_all(blocks, 'hop', split_axis=0, concat_axis=0, tiled=True)  30.2 us
  transfers between devices with their start and end apart: 11, of which 9 were waited for; matrix products, arithmetic and copies ran while one was open for 27% of the time, Pallas kernels for 3%

profile of v2, /device:TPU:0, one launch (start us, length us, event | category | flops | bytes accessed | tf_op | source)
XLA Modules:
  0.0 787.4 jit_solution(7512727219716733479)
XLA Ops:
  9.9 10.9 %multiply_reduce_fusion = f32[]{:T(128)} fusion(bf16[1,1024,8192]{2,1,0:T(8,128)(2,1)} %param.16), kind=kLoop, calls=%fused_computation | loop fusion | flops 25165824 | bytes 16777220 | tf_op jit(solution)/shard_map/reduce_sum | solution.py:101
  22.5 7.3 all-to-all-start
  29.8 7.2 all-gather.1
  37.0 16.4 %all-to-all-done.in_ref = bf16[8,112,256]{2,1,0:T(8,128)(2,1)S(1)} async-done(((bf16[8,112,256]{2,1,0:T(8,128)(2,1)}), bf16[8,112,256]{2,1,0:T(8,128)(2,1)S(1)}, u32[]{:S(2)}, u32[]{:S(2)}) %all-to-all-start) | async-done | bytes 458784 | tf_op jit(solution)/shard_map/all_to_all | solution.py:70
  54.2 5.3 shard_map.113
  59.5 3.5 all-to-all-start.1
  63.0 11.8 %fusion.27 = bf16[256,8192]{1,0:T(8,128)(2,1)} fusion(bf16[1,1024,8192]{2,1,0:T(8,128)(2,1)} %param.16, bf16[1,256,1024]{2,1,0:T(8,128)(2,1)S(1)} %all-gather.1), kind=kOutput, calls=%fused_computation.31 | convolution fusion | flops 4297064448 | bytes 21495808 | tf_op jit(solution)/shard_map/dot_general | solution.py:23
  74.8 7.1 all_gather.33
  83.4 4.6 all-to-all-start.2
  88.1 11.9 %fusion.30 = bf16[256,8192]{1,0:T(8,128)(2,1)} fusion(bf16[256,1024]{1,0:T(8,128)(2,1)S(1)} %all_gather.33, bf16[1,1024,8192]{2,1,0:T(8,128)(2,1)} %param.16), kind=kOutput, calls=%fused_computation.32 | convolution fusion | flops 4297064448 | bytes 21495808 | tf_op jit(solution)/shard_map/dot_general | solution.py:23
  102.5 7.6 all_gather.34
  111.3 12.4 %fusion = f32[256,8192]{1,0:T(8,128)} fusion(bf16[256,1024]{1,0:T(8,128)(2,1)S(1)} %all_gather.34, bf16[1,1024,8192]{2,1,0:T(8,128)(2,1)} %param.14), kind=kOutput, calls=%fused_computation.1 | convolution fusion | flops 4294967296 | bytes 25690112 | tf_op jit(solution)/shard_map/dot_general | solution.py:23
  123.8 216.1 %all-gather.6.cloned.1.call-done = bf16[8192,1024]{1,0:T(8,128)(2,1)} async-done(((bf16[8192,128]{1,0:T(8,128)(2,1)}), bf16[8192,1024]{1,0:T(8,128)(2,1)}) %all-gather.6.cloned.1.call-update) | async-done | bytes 16777232 | tf_op jit(solution)/shard_map/all_gather | solution.py:91
  339.9 14.4 %fusion.49 = f32[256,1024]{1,0:T(8,128)} fusion(bf16[8192,1024]{1,0:T(8,128)(2,1)} %all-gather.6.cloned.1.call-done, f32[256,8192]{1,0:T(8,128)} %fusion), kind=kOutput, calls=%fused_computation.59 | convolution fusion | flops 4313841664 | bytes 26214400 | tf_op jit(solution)/shard_map/dot_general | solution.py:23
  354.3 7.2 all-gather
  361.5 7.3 all_gather.31
  369.3 15.8 %fusion.2 = f32[512,8192]{1,0:T(8,128)} fusion(bf16[1,1024,8192]{2,1,0:T(8,128)(2,1)} %param.14, bf16[256,1024]{1,0:T(8,128)(2,1)S(1)} %all_gather.31, bf16[256,1024]{1,0:T(8,128)(2,1)S(1)} %bitcast.99), kind=kOutput, calls=%fused_computation.3 | convolution fusion | flops 8592031744 | bytes 34603008 | tf_op jit(solution)/shard_map/dot_general | solution.py:23
  386.2 7.5 all_gather.36
  393.6 5.5 all-to-all-start.4
  399.2 15.7 %multiply_reduce_fusion.2 = (f32[256]{0:T(256)S(1)}, f32[256,8192]{1,0:T(8,128)}) fusion(f32[256,8192]{1,0:T(8,128)} %fusion, bf16[256,1024]{1,0:T(8,128)(2,1)S(1)} %all_gather.36, bf16[8192,1024]{1,0:T(8,128)(2,1)} %all-gather.6.cloned.1.call-done), kind=kOutput, calls=%fused_computation.56 | convolution fusion | flops 4336910336 | bytes 34079744 | tf_op jit(solution)/shard_map/dot_general | solution.py:27
  414.8 7.0 psum.28
  426.9 12.6 %fusion.24 = f32[256,8192]{1,0:T(8,128)} fusion(bf16[256,1024]{1,0:T(8,128)(2,1)S(1)} %all_gather.34, bf16[1,1024,8192]{2,1,0:T(8,128)(2,1)} %param.16, f32[]{:T(128)S(6)} %mul.307), kind=kOutput, calls=%fused_computation.30 | convolution fusion | flops 4301258752 | bytes 25690116 | tf_op jit(solution)/shard_map/dot_general | solution.py:23
  440.5 2.0 copy-done
  442.5 7.0 fusion.61
  450.1 7.3 shard_map.114
  457.4 6.8 psum.29
  465.5 13.7 %fusion.48 = f32[512,8192]{1,0:T(8,128)} fusion(bf16[256,8192]{1,0:T(8,128)(2,1)} %copy-done, bf16[512,256]{0,1:T(8,128)(2,1)S(1)} %get-tuple-element.28, bf16[512,256]{0,1:T(8,128)(2,1)S(1)} %get-tuple-element.29), kind=kOutput, calls=%fused_computation.58 | convolution fusion | flops 4312793088 | bytes 21495808 | tf_op jit(solution)/shard_map/dot_general | solution.py:23
  479.2 13.7 %all-to-all-done.4.in_ref = bf16[8,32,8192]{2,1,0:T(8,128)(2,1)} async-done(((bf16[8,32,8192]{2,1,0:T(8,128)(2,1)}), bf16[8,32,8192]{2,1,0:T(8,128)(2,1)}, u32[]{:S(2)}, u32[]{:S(2)}) %all-to-all-start.4) | async-done | bytes 4194336 | tf_op jit(solution)/shard_map/all_to_all | solution.py:70
  492.9 4.6 all-to-all-start.3
  497.6 26.3 %multiply_subtract_fusion = f32[512,8192]{1,0:T(8,128)} fusion(f32[512,8192]{1,0:T(8,128)} %fusion.2, f32[512,8192]{1,0:T(8,128)} %fusion.48, bf16[1,1024,8192]{2,1,0:T(8,128)(2,1)} %param.16, f32[]{:T(128)S(6)} %mul.306, f32[]{:T(128)S(6)} %mul.313, bf16[256,1024]{1,0:T(8,128)(2,1)S(1)} %all_gather.31, bf16[256,1024]{1,0:T(8,128)(2,1)S(1)} %bitcast.100), kind=kOutput, calls=%fused_computation.13 | convolution fusion | flops 8608808960 | bytes 68157448 | tf_op jit(solution)/shard_map/dot_general | solution.py:23
  523.8 14.4 %fusion.50 = f32[256,1024]{1,0:T(8,128)} fusion(bf16[8192,1024]{1,0:T(8,128)(2,1)} %all-gather.6.cloned.1.call-done, f32[512,8192]{1,0:T(8,128)} %multiply_subtract_fusion), kind=kOutput, calls=%fused_computation.60 | convolution fusion | flops 4313841664 | bytes 26214400 | tf_op jit(solution)/shard_map/dot_general | solution.py:23
  540.1 7.3 shard_map.115
  547.4 16.9 %reduce-scatter.6.cloned.1.call-done = f32[256,256]{1,0:T(8,128)} async-done(((f32[256,1024]{1,0:T(8,128)}), f32[256,256]{1,0:T(8,128)}) %reduce-scatter.6.cloned.1.call-update) | async-done | bytes 262160 | tf_op jit(solution)/shard_map/reduce_scatter | solution.py:130
  565.4 6.8 all_gather.37
  572.2 18.2 %all-to-all-done.3 = bf16[8,32,8192]{2,1,0:T(8,128)(2,1)} async-done(((bf16[8,32,8192]{2,1,0:T(8,128)(2,1)}), bf16[8,32,8192]{2,1,0:T(8,128)(2,1)}, u32[]{:S(2)}, u32[]{:S(2)}) %all-to-all-start.3) | async-done | bytes 4194336 | tf_op jit(solution)/shard_map/all_to_all | solution.py:71
  590.4 4.6 all-to-all-start.5
  595.2 15.7 %multiply_reduce_fusion.1 = (f32[256]{0:T(256)S(1)}, f32[256,8192]{1,0:T(8,128)}) fusion(f32[512,8192]{1,0:T(8,128)} %multiply_subtract_fusion, bf16[256,1024]{1,0:T(8,128)(2,1)S(1)} %all_gather.37, bf16[8192,1024]{1,0:T(8,128)(2,1)} %all-gather.6.cloned.1.call-done), kind=kOutput, calls=%fused_computation.53 | convolution fusion | flops 4336910336 | bytes 34079744 | tf_op jit(solution)/shard_map/dot_general | solution.py:27
  610.9 6.1 psum.30
  620.2 3.3 convert_multiply_fusion.1
  624.8 2.9 multiply_convert_fusion
  627.7 7.8 fusion.62
  636.5 6.9 psum.31
  644.7 42.8 %all-to-all-done.5 = bf16[8,32,8192]{2,1,0:T(8,128)(2,1)} async-done(((bf16[8,32,8192]{2,1,0:T(8,128)(2,1)}), bf16[8,32,8192]{2,1,0:T(8,128)(2,1)}, u32[]{:S(2)}, u32[]{:S(2)}) %all-to-all-start.5) | async-done | bytes 4194336 | tf_op jit(solution)/shard_map/all_to_all | solution.py:71
  687.5 6.4 convert_multiply_fusion
  693.8 16.9 %fusion.57 = f32[256,1024]{1,0:T(8,128)} fusion(bf16[8192,1024]{1,0:T(8,128)(2,1)} %all-gather.6.cloned.1.call-done, f32[256,8192]{1,0:T(8,128)} %bitcast.97, f32[512,8192]{1,0:T(8,128)} %multiply_subtract_fusion, bf16[256,8192]{1,0:T(8,128)(2,1)} %multiply_convert_fusion, f32[]{:T(128)S(6)} %mul.350, bf16[256,256]{0,1:T(8,128)(2,1)S(1)} %get-tuple-element.20, ...), kind=kOutput, calls=%fused_computation.67 | convolution fusion | flops 6484918272 | bytes 39059460 | tf_op jit(solution)/shard_map/dot_general | solution.py:23
  710.9 23.8 %reduce-scatter.8.cloned.1.call-done = f32[256,256]{1,0:T(8,128)} async-done(((f32[256,1024]{1,0:T(8,128)}), f32[256,256]{1,0:T(8,128)}) %reduce-scatter.8.cloned.1.call-update) | async-done | bytes 262160 | tf_op jit(solution)/shard_map/reduce_scatter | solution.py:130
  738.9 38.6 %all-gather.8.cloned.1.call-done = bf16[2176,256]{1,0:T(8,128)(2,1)} async-done(((bf16[272,256]{1,0:T(8,128)(2,1)}), bf16[2176,256]{1,0:T(8,128)(2,1)}) %all-gather.8.cloned.1.call-update) | async-done | bytes 1114128 | tf_op jit(solution)/shard_map/all_gather | solution.py:175
  777.6 1.6 dynamic-slice_bitcast_fusion
  (82 shorter events, 22.7 us)
Async XLA Ops:
  7.2 332.8 %all-gather.6.cloned.1.call-start = ((), (), s32[]{:S(2)}) async-start(), calls=%async_computation.9 | async-start | bytes 18874368 | tf_op jit(solution)/shard_map/all_gather | solution.py:91
  9.9 11.7 %slice-start = ((bf16[3,256,256]{2,1,0:T(8,128)(2,1)}), bf16[2,256,256]{2,1,0:T(8,128)(2,1)S(1)}, s32[]{:S(2)}) async-start(bf16[3,256,256]{2,1,0:T(8,128)(2,1)} %param.12), calls=%async_computation.14 | async-start | bytes 524288 | tf_op jit(solution)/shard_map/slice | solution.py:104
  9.9 11.7 %slice-start.1 = ((bf16[2,256,256]{2,1,0:T(8,128)(2,1)}), bf16[1,256,256]{2,1,0:T(8,128)(2,1)S(1)}, s32[]{:S(2)}) async-start(bf16[2,256,256]{2,1,0:T(8,128)(2,1)} %param.13), calls=%async_computation.15 | async-start | bytes 262144 | tf_op jit(solution)/shard_map/slice | solution.py:104
  9.9 19.9 %copy-start.4 = (bf16[3,256,256]{2,1,0:T(8,128)(2,1)S(1)}, bf16[3,256,256]{2,1,0:T(8,128)(2,1)}, u32[]{:S(2)}) copy-start(bf16[3,256,256]{2,1,0:T(8,128)(2,1)} %param.12) | copy-start | bytes 1179652
  22.5 30.9 %all-to-all-start = ((bf16[8,112,256]{2,1,0:T(8,128)(2,1)}), bf16[8,112,256]{2,1,0:T(8,128)(2,1)S(1)}, u32[]{:S(2)}, u32[]{:S(2)}) async-start(bf16[8,112,256]{2,1,0:T(8,128)(2,1)} %pad_maximum_fusion.13), calls=%async_computation | async-start | bytes 917504 | tf_op jit(solution)/shard_map/all_to_all | solution.py:70
  53.4 0.8 copy-start.3
  59.5 23.9 %all-to-all-start.1 = ((bf16[8,112,256]{2,1,0:T(8,128)(2,1)}), bf16[8,112,256]{2,1,0:T(8,128)(2,1)S(1)}, u32[]{:S(2)}, u32[]{:S(2)}) async-start(bf16[8,112,256]{2,1,0:T(8,128)(2,1)} %shard_map.113), calls=%async_computation.1 | async-start | bytes 917504 | tf_op jit(solution)/shard_map/all_to_all | solution.py:71
  83.4 310.2 %all-to-all-start.2 = ((bf16[8,32,8192]{2,1,0:T(8,128)(2,1)}), bf16[8,32,8192]{2,1,0:T(8,128)(2,1)}, u32[]{:S(2)}, u32[]{:S(2)}) async-start(bf16[8,32,8192]{2,1,0:T(8,128)(2,1)} %bitcast.102), calls=%async_computation.4 | async-start | bytes 8388608 | tf_op jit(solution)/shard_map/all_to_all | solution.py:70
  88.0 12.7 %copy-start.9 = (f32[8]{0:T(128)S(1)}, f32[8]{0:T(128)}, u32[]{:S(2)}) copy-start(f32[8]{0:T(128)} %param.18) | copy-start | bytes 100
  88.0 13.3 %copy-start.10 = (f32[8]{0:T(128)S(1)}, f32[8]{0:T(128)}, u32[]{:S(2)}) copy-start(f32[8]{0:T(128)} %param.19) | copy-start | bytes 100
  88.0 13.8 %copy-start.11 = (f32[8]{0:T(128)S(1)}, f32[8]{0:T(128)}, u32[]{:S(2)}) copy-start(f32[8]{0:T(128)} %param.17) | copy-start | bytes 100
  88.0 297.1 %reduce-scatter.4.cloned.1.call-start = ((), (), s32[]{:S(2)}) async-start(), calls=%async_computation.10 | async-start | bytes 1310720 | tf_op jit(solution)/shard_map/reduce_scatter | solution.py:130
  369.3 15.8 %copy-start.5 = (bf16[2,256,256]{2,1,0:T(8,128)(2,1)S(1)}, bf16[2,256,256]{2,1,0:T(8,128)(2,1)}, u32[]{:S(2)}) copy-start(bf16[2,256,256]{2,1,0:T(8,128)(2,1)} %param.13) | copy-start | bytes 786436
  393.6 99.3 %all-to-all-start.4 = ((bf16[8,32,8192]{2,1,0:T(8,128)(2,1)}), bf16[8,32,8192]{2,1,0:T(8,128)(2,1)}, u32[]{:S(2)}, u32[]{:S(2)}) async-start(bf16[8,32,8192]{2,1,0:T(8,128)(2,1)} %bitcast.101), calls=%async_computation.6 | async-start | bytes 8388608 | tf_op jit(solution)/shard_map/all_to_all | solution.py:70
  426.9 12.6 %copy-start.2 = (f32[256,8192]{1,0:T(8,128)S(1)}, f32[256,8192]{1,0:T(8,128)}, u32[]{:S(2)}) copy-start(f32[256,8192]{1,0:T(8,128)} %get-tuple-element.53) | copy-start | bytes 25165828
  439.6 2.9 copy-start.6
  439.6 2.9 copy-start.7
  440.5 2.0 copy-start
  492.9 97.4 %all-to-all-start.3 = ((bf16[8,32,8192]{2,1,0:T(8,128)(2,1)}), bf16[8,32,8192]{2,1,0:T(8,128)(2,1)}, u32[]{:S(2)}, u32[]{:S(2)}) async-start(bf16[8,32,8192]{2,1,0:T(8,128)(2,1)} %shard_map.114), calls=%async_computation.5 | async-start | bytes 8388608 | tf_op jit(solution)/shard_map/all_to_all | solution.py:71
  497.5 66.8 %reduce-scatter.6.cloned.1.call-start = ((), (), s32[]{:S(2)}) async-start(), calls=%async_computation.11 | async-start | bytes 1310720 | tf_op jit(solution)/shard_map/reduce_scatter | solution.py:130
  590.4 97.1 %all-to-all-start.5 = ((bf16[8,32,8192]{2,1,0:T(8,128)(2,1)}), bf16[8,32,8192]{2,1,0:T(8,128)(2,1)}, u32[]{:S(2)}, u32[]{:S(2)}) async-start(bf16[8,32,8192]{2,1,0:T(8,128)(2,1)} %shard_map.115), calls=%async_computation.7 | async-start | bytes 8388608 | tf_op jit(solution)/shard_map/all_to_all | solution.py:71
  594.9 139.7 %reduce-scatter.8.cloned.1.call-start = ((), (), s32[]{:S(2)}) async-start(), calls=%async_computation.12 | async-start | bytes 1310720 | tf_op jit(solution)/shard_map/reduce_scatter | solution.py:130
  620.2 4.6 copy-start.1
  693.8 42.5 %copy-start.8 = (s32[8]{0:T(128)S(1)}, s32[8]{0:T(128)}, u32[]{:S(2)}) copy-start(s32[8]{0:T(128)} %order_ref.5) | copy-start | bytes 100
  710.8 66.8 %all-gather.8.cloned.1.call-start = ((), (), s32[]{:S(2)}) async-start(), calls=%async_computation.13 | async-start | bytes 1253376 | tf_op jit(solution)/shard_map/all_gather | solution.py:175
Sparse Core Ops, SparseCore 0:
  10.0 329.8 all-gather.5
  354.5 25.8 reduce-scatter.3
  538.4 25.9 reduce-scatter.5
  710.9 23.6 reduce-scatter.7
  736.9 40.6 all-gather.7
